TPU v7x, 32 devices: a whole 2x2x4 slice. The times are simulated.
32 devices in a mesh: chan: 8 (over z, y), ctr: 4 (over x, core).
Axes of the slice: x: 2, y: 2, z: 4, core: 2. Of those that a mesh axis runs over, the one named last changes fastest.
Arguments:
- amplitudes: float32 [4608, 8, 256], P('ctr', 'chan'), may hold values from -6 to 6
- pair_interaction: bfloat16 [8, 4608, 4608], P('chan', None, 'ctr'), may hold values from -0.09375 to 0.09375
- ph_interaction: float32 [16, 128, 128], P('chan'), may hold values from -0.5 to 0.5
- pp_size: int32 [8], P('chan'), may hold values from 1 to 72, as said below
- ph_owner: int32 [72, 8, 2], P('ctr', 'chan'), may hold values from 0 to 15, as said below
Outputs:
- residual: float32 [4608, 8, 256], P('ctr', 'chan')
Inputs may be any that keep to these rules, and one draw needn't show every extreme that they name: Channel c has its first 64 * pp_size[c] particle pairs live; every draw has a channel with 72 live tiles. `ph_owner`: the ph channel g is owned by index g // 2 of chan. Of the 36 tiles that one device holds, at most 9 have ph channels owned by one index of chan; in every draw some index of chan receives exactly 9 tiles from every device.
All inputs are finite; a program needn't handle non-finite values.
Results may differ from a plain program's by a relative error of at most 0.002.
Values may be sent and summed in bfloat16 or wider, within the bound.
A program may use at most 128 MiB of HBM per device.

v0:
```python
import jax
import jax.numpy as jnp
from jax import lax
from jax.sharding import PartitionSpec as P


def local(amplitudes, pair_interaction, ph_interaction, pp_size, ph_owner):
    row_count, chan_count, hole_width = amplitudes.shape
    row_tiles, _, col_tiles = ph_owner.shape
    tile_rows = row_count // row_tiles
    tile_cols = hole_width // col_tiles
    offset = lax.axis_index("ctr") * row_count
    positions = offset + jnp.arange(row_count, dtype=jnp.int32)
    live_mask = positions[:, None] < (pp_size * tile_rows)[None, :]
    masked = jnp.where(live_mask[:, :, None], amplitudes, jnp.zeros_like(amplitudes))
    lowered = masked.astype(jnp.bfloat16)
    ladder = lax.psum_scatter(
        jnp.einsum("crk,kch->rch", pair_interaction, lowered, preferred_element_type=jnp.float32),
        "ctr",
        scatter_dimension=0,
        tiled=True,
    )
    tile_count = row_tiles * chan_count * col_tiles
    tile_data = masked.reshape(row_tiles, tile_rows, chan_count, col_tiles, tile_cols)
    tile_data = jnp.transpose(tile_data, (0, 2, 3, 1, 4)).reshape(tile_count, tile_rows, tile_cols)
    owners = ph_owner.reshape(tile_count)
    chan_size = lax.axis_size("chan")
    capacity = max(2, 2 * tile_count // chan_size)
    per_owner = ph_interaction.shape[0]
    target = owners // per_owner
    onehot = (target[:, None] == jnp.arange(chan_size, dtype=jnp.int32)[None, :]).astype(jnp.int32)
    slot_rank = jnp.sum((jnp.cumsum(onehot, axis=0) - onehot) * onehot, axis=1)
    slot = target * capacity + slot_rank
    outgoing = (
        jnp.zeros((chan_size * capacity, tile_rows, tile_cols), jnp.float32).at[slot].set(tile_data)
    )
    outgoing = outgoing.reshape(chan_size, capacity, tile_rows, tile_cols)
    channel_ids = (
        jnp.zeros((chan_size * capacity,), jnp.int32)
        .at[slot]
        .set(owners)
        .reshape(chan_size, capacity)
    )
    block = lax.all_to_all(outgoing, "chan", split_axis=0, concat_axis=0, tiled=True)
    labels = lax.all_to_all(channel_ids, "chan", split_axis=0, concat_axis=0, tiled=True)
    local_ids = labels % per_owner
    result = jnp.zeros_like(block)
    for which in range(per_owner):
        product = jnp.einsum(
            "abst,tu->absu", block, ph_interaction[which], precision=lax.Precision.HIGHEST
        )
        result = jnp.where((local_ids == which)[:, :, None, None], product, result)
    returned = lax.all_to_all(result, "chan", split_axis=0, concat_axis=0, tiled=True)
    returned = returned.reshape(chan_size * capacity, tile_rows, tile_cols)
    cycle_tiles = returned[slot]
    cycle = cycle_tiles.reshape(row_tiles, chan_count, col_tiles, tile_rows, tile_cols)
    cycle = jnp.transpose(cycle, (0, 3, 1, 2, 4)).reshape(row_count, chan_count, hole_width)
    return jnp.where(live_mask[:, :, None], ladder, jnp.zeros_like(ladder)) + cycle


def solution(mesh):
    in_specs = (
        P("ctr", "chan", None),
        P("chan", None, "ctr"),
        P("chan", None, None),
        P("chan"),
        P("ctr", "chan", None),
    )
    out_specs = P("ctr", "chan", None)
    return jax.shard_map(local, mesh=mesh, in_specs=in_specs, out_specs=out_specs, check_vma=False)
```

profile of v0, /device:TPU:0, one launch (start us, length us, event | category | flops | bytes accessed | tf_op | source)
XLA Modules:
  0.0 174.9 jit_solution(12850595864707575727)
XLA Ops:
  7.2 2.6 %copy.18 = f32[1152,1,256]{0,2,1:T(8,128)S(1)} copy(f32[1152,1,256]{2,1,0:T(1,128)} %param.5) | data formatting | bytes 2359296 | tf_op args[0]
  9.8 0.1 broadcast_select_fusion
  9.9 12.3 %fusion.2 = f32[4608,1,256]{0,2,1:T(8,128)} fusion(bf16[1,4608,1152]{2,1,0:T(8,128)(2,1)} %param.6, f32[1152,1,256]{0,2,1:T(8,128)S(1)} %broadcast_select_fusion), kind=kOutput, calls=%fused_computation.5 | convolution fusion | flops 2718203904 | bytes 16515072 | tf_op jit(solution)/shard_map/crk,kch->rch/dot_general | solution.py:18
  22.3 0.0 reduce-scatter.2.cloned.1.call-update
  22.3 0.7 copy-done.2
  22.9 0.1 copy.19
  23.0 0.1 reshape.196
  23.1 0.1 fusion.12
  23.2 0.1 reshape.176
  23.3 0.1 reduce_window_sum.11
  23.4 0.2 select_reduce_fusion
  23.6 0.7 scatter_custom_fusion
  24.3 0.7 all_to_all.14
  24.9 7.3 %all-to-all-start = ((s32[8,1,9]{2,1,0:T(1,128)}), s32[8,1,9]{2,1,0:T(1,128)S(1)}, u32[]{:S(2)}, u32[]{:S(2)}) async-start(s32[8,1,9]{2,1,0:T(1,128)} %bitcast.7), calls=%async_computation.1 | async-start | bytes 8192 | tf_op jit(solution)/shard_map/all_to_all | solution.py:45
  32.2 1.9 %copy.22 = f32[1152,1,256]{2,1,0:T(1,128)S(1)} copy(f32[1152,1,256]{0,2,1:T(8,128)S(1)} %broadcast_select_fusion) | data formatting | bytes 2359296 | tf_op jit(solution)/shard_map/jit(_where)/select_n | solution.py:15
  34.2 0.1 copy.23
  34.3 0.3 broadcast_in_dim.47
  34.6 2.3 %scatter_fusion = f32[72,64,128]{2,1,0:T(8,128)S(1)} fusion(f32[72,64,128]{2,1,0:T(8,128)S(1)} %broadcast_in_dim.47, s32[36]{0:T(128)S(1)} %fusion.14, f32[36,64,128]{2,1,0:T(8,128)S(1)} %bitcast.56), kind=kCustom, calls=%fused_computation.2 | custom fusion | bytes 3539088 | tf_op jit(solution)/shard_map/scatter | solution.py:35
  36.9 1.7 all-to-all-done
  38.6 0.0 copy-done
  38.6 5.8 %all-to-all-start.1 = ((f32[8,9,64,128]{3,2,1,0:T(8,128)}), f32[8,9,64,128]{3,2,1,0:T(8,128)S(1)}, u32[]{:S(2)}, u32[]{:S(2)}) async-start(f32[8,9,64,128]{3,2,1,0:T(8,128)} %bitcast.51), calls=%async_computation.2 | async-start | bytes 4718592 | tf_op jit(solution)/shard_map/all_to_all | solution.py:44
  44.5 53.3 %all-to-all-done.1 = f32[8,9,64,128]{3,2,1,0:T(8,128)S(1)} async-done(((f32[8,9,64,128]{3,2,1,0:T(8,128)}), f32[8,9,64,128]{3,2,1,0:T(8,128)S(1)}, u32[]{:S(2)}, u32[]{:S(2)}) %all-to-all-start.1) | async-done | bytes 2359328 | tf_op jit(solution)/shard_map/all_to_all | solution.py:44
  97.8 2.1 %fusion.8 = f32[8,9,64,128]{3,2,1,0:T(8,128)S(1)} fusion(f32[8,9,64,128]{3,2,1,0:T(8,128)S(1)} %all-to-all-done.1, f32[2,128,128]{2,1,0:T(8,128)S(1)} %copy-done.1), kind=kOutput, calls=%fused_computation.12 | convolution fusion | flops 905969664 | bytes 4784128 | tf_op jit(solution)/shard_map/abst,tu->absu/dot_general | solution.py:49
  99.9 3.5 %select_select_fusion = f32[8,9,64,128]{3,2,1,0:T(8,128)} fusion(f32[8,9,64,128]{3,2,1,0:T(8,128)S(1)} %fusion.8, f32[8,9,64,128]{3,2,1,0:T(8,128)S(1)} %all-to-all-done.1, pred[8,9]{1,0:T(8,128)(4,1)S(1)} %get-tuple-element.6, pred[8,9]{1,0:T(8,128)(4,1)S(1)} %get-tuple-element.5, f32[2,128,128]{2,1,0:T(8,128)S(1)} %copy-done.1), kind=kOutput, calls=%fused_computation.6 | convolution fusion | flops 907149312 | bytes 7145472 | tf_op jit(solution)/shard_map/abst,tu->absu/dot_general | solution.py:49
  103.4 3.6 %all-to-all-start.2 = ((f32[8,9,64,128]{3,2,1,0:T(8,128)}), f32[8,9,64,128]{3,2,1,0:T(8,128)S(1)}, u32[]{:S(2)}, u32[]{:S(2)}) async-start(f32[8,9,64,128]{3,2,1,0:T(8,128)} %select_select_fusion), calls=%async_computation.3 | async-start | bytes 4718592 | tf_op jit(solution)/shard_map/all_to_all | solution.py:53
  107.0 54.0 %all-to-all-done.2 = f32[8,9,64,128]{3,2,1,0:T(8,128)S(1)} async-done(((f32[8,9,64,128]{3,2,1,0:T(8,128)}), f32[8,9,64,128]{3,2,1,0:T(8,128)S(1)}, u32[]{:S(2)}, u32[]{:S(2)}) %all-to-all-start.2) | async-done | bytes 2359328 | tf_op jit(solution)/shard_map/all_to_all | solution.py:53
  161.0 0.6 gather_fusion
  161.6 0.9 copy.24
  162.6 1.9 %copy.25 = f32[1152,1,256]{0,2,1:T(8,128)S(1)} copy(f32[1152,1,256]{2,1,0:T(1,128)S(1)} %bitcast.55) | data formatting | bytes 2359296 | tf_op jit(solution)/shard_map/reshape | solution.py:57
  164.5 0.0 reduce-scatter.2.cloned.1.call-done
  164.5 1.4 select_add_fusion
  165.9 2.1 %copy.26 = f32[1152,1,256]{2,1,0:T(1,128)} copy(f32[1152,1,256]{0,2,1:T(8,128)S(1)} %select_add_fusion) | data formatting | bytes 2359296 | tf_op jit(solution)/shard_map/add | solution.py:58
  (10 shorter events, 0.1 us)
Async XLA Ops:
  6.5 158.0 %reduce-scatter.2.cloned.1.call-start = ((), (), s32[]{:S(2)}) async-start(), calls=%async_computation.4 | async-start | bytes 5898240 | tf_op jit(solution)/shard_map/reduce_scatter | solution.py:17
  22.3 0.7 copy-start.2
  24.9 13.7 %all-to-all-start = ((s32[8,1,9]{2,1,0:T(1,128)}), s32[8,1,9]{2,1,0:T(1,128)S(1)}, u32[]{:S(2)}, u32[]{:S(2)}) async-start(s32[8,1,9]{2,1,0:T(1,128)} %bitcast.7), calls=%async_computation.1 | async-start | bytes 8192 | tf_op jit(solution)/shard_map/all_to_all | solution.py:45
  36.9 1.7 copy-start
  38.6 59.2 %copy-start.1 = (f32[2,128,128]{2,1,0:T(8,128)S(1)}, f32[2,128,128]{2,1,0:T(8,128)}, u32[]{:S(2)}) copy-start(f32[2,128,128]{2,1,0:T(8,128)} %param.7) | copy-start | bytes 393220
  38.6 59.2 %all-to-all-start.1 = ((f32[8,9,64,128]{3,2,1,0:T(8,128)}), f32[8,9,64,128]{3,2,1,0:T(8,128)S(1)}, u32[]{:S(2)}, u32[]{:S(2)}) async-start(f32[8,9,64,128]{3,2,1,0:T(8,128)} %bitcast.51), calls=%async_computation.2 | async-start | bytes 4718592 | tf_op jit(solution)/shard_map/all_to_all | solution.py:44
  103.4 57.6 %all-to-all-start.2 = ((f32[8,9,64,128]{3,2,1,0:T(8,128)}), f32[8,9,64,128]{3,2,1,0:T(8,128)S(1)}, u32[]{:S(2)}, u32[]{:S(2)}) async-start(f32[8,9,64,128]{3,2,1,0:T(8,128)} %select_select_fusion), calls=%async_computation.3 | async-start | bytes 4718592 | tf_op jit(solution)/shard_map/all_to_all | solution.py:53
Sparse Core Ops, SparseCore 0:
  22.4 50.5 reduce-scatter.1
where the time goes:
time: 175 us
  waiting for transfers between devices  109 us (62%)
  matrix products  17.9 us (10%)
  starting transfers between devices  16.7 us (10%)
  local copies, waits for them, and re-layouts  15.1 us (9%)
  between operations  14.2 us (8%)
  other arithmetic  1.84 us (1%)
    all_to_all x1, waiting for transfers between devices, local(): lax.all_to_all(result, 'chan', split_axis=0, concat_axis=0, tiled=True)  54 us
    all_to_all x1, waiting for transfers between devices, local(): lax.all_to_all(outgoing, 'chan', split_axis=0, concat_axis=0, tiled=True)  53.3 us
    dot_general x1, matrix products, local(): jnp.einsum('crk,kch->rch', pair_interaction, lowered, preferred_element_t...  12.3 us
    all_to_all x1, starting transfers between devices, local(): lax.all_to_all(channel_ids, 'chan', split_axis=0, concat_axis=0, tiled=True)  7.28 us
    all_to_all x1, starting transfers between devices, local(): lax.all_to_all(outgoing, 'chan', split_axis=0, concat_axis=0, tiled=True)  5.84 us
    dot_general x2, matrix products, local(): jnp.einsum('abst,tu->absu', block, ph_interaction[which], precision=lax.P...  5.58 us
    all_to_all x1, starting transfers between devices, local(): lax.all_to_all(result, 'chan', split_axis=0, concat_axis=0, tiled=True)  3.61 us
  transfers between devices with their start and end apart: 4, of which 3 were waited for; matrix products, arithmetic and copies ran while one was open for 9% of the time, Pallas kernels for 0%

commit v1 on v0

v1 whole, which is shorter than its diff:
```python
import functools

import jax
import jax.numpy as jnp
from jax import lax
from jax.experimental import pallas as pl
from jax.experimental.pallas import tpu as pltpu
from jax.sharding import PartitionSpec as P

MESH = pl.DeviceIdType.MESH


def split(x):
    head = x.astype(jnp.bfloat16)
    return head, (x - head.astype(jnp.float32)).astype(jnp.bfloat16)


def kernel(
    dims,
    size_ref,
    owner_ref,
    amp_hbm,
    w_hbm,
    ph_hbm,
    out_hbm,
    amp,
    wbuf,
    low,
    part,
    sib_buf,
    x_send,
    x_recv,
    ph_all,
    out,
    amp_sem,
    w_sem,
    ph_sem,
    out_sem,
    sib_send_sem,
    sib_recv_sem,
    x_send_sem,
    x_recv_sem,
    z_send_sem,
    z_recv_sem,
    y_send_sem,
    y_recv_sem,
    p_send_sem,
    p_recv_sem,
):
    n_hi, n_chunk, chunk, rows, tile, tiles, per_owner = dims
    chan = lax.axis_index("chan")
    ctr = lax.axis_index("ctr")
    hi, lo = chan // 2, lax.rem(chan, 2)
    pair, core = ctr // 2, lax.rem(ctr, 2)
    half = per_owner // 2
    sibling = (chan, pair * 2 + 1 - core)
    across = (chan, (1 - pair) * 2 + core)
    beside = (hi * 2 + 1 - lo, ctr)

    def along(step):
        return (lax.rem(hi + step, n_hi) * 2 + lo, ctr)

    barrier = pltpu.get_barrier_semaphore()
    for device in (sibling, across, beside):
        pl.semaphore_signal(barrier, inc=1, device_id=device, device_id_type=MESH)

    @pl.loop(1, n_hi)
    def _(step):
        pl.semaphore_signal(barrier, inc=1, device_id=along(step), device_id_type=MESH)

    amp_copy = pltpu.make_async_copy(amp_hbm, amp, amp_sem)
    amp_copy.start()
    ph_copy = pltpu.make_async_copy(
        ph_hbm, ph_all.at[pl.ds(chan * per_owner, per_owner)], ph_sem
    )
    ph_copy.start()

    def w_copy(j, side):
        far = 1 - j // n_chunk
        owner_pair = pair + far * (1 - 2 * pair)
        owner_core = core + (1 - side) * (1 - 2 * core)
        start = (owner_pair * 2 + owner_core) * rows + lax.rem(j, n_chunk) * chunk
        return pltpu.make_async_copy(
            w_hbm.at[pl.ds(pl.multiple_of(start, chunk), chunk)],
            wbuf.at[j, pl.ds(side * chunk, chunk)],
            w_sem.at[j, side],
        )

    @pl.loop(0, 2 * n_chunk)
    def _(j):
        w_copy(j, 0).start()
        w_copy(j, 1).start()

    live = size_ref[0] * tile - ctr * rows

    def live_mask(start, count):
        return start + lax.broadcasted_iota(jnp.int32, (count, 128), 0) < live

    amp_copy.wait()

    @pl.loop(0, tiles)
    def _(r):
        mask = live_mask(r * tile, tile)
        for h in range(2):
            value = amp[pl.ds(r * 2 * tile + h, tile, 2), :]
            low[pl.ds(pl.multiple_of(r * tile, tile), tile), h * 128 : (h + 1) * 128] = (
                jnp.where(mask, value, jnp.zeros_like(value)).astype(jnp.bfloat16)
            )

    ph_copy.wait()
    pl.semaphore_wait(barrier, n_hi + 2)

    def ph_slot(owner, which):
        return ph_all.at[pl.ds(owner * per_owner + which * half, half)]

    def remote(ref, device, send_sem, recv_sem):
        return pltpu.make_async_remote_copy(
            src_ref=ref,
            dst_ref=ref,
            send_sem=send_sem,
            recv_sem=recv_sem,
            device_id=device,
            device_id_type=MESH,
        )

    def z_copy(step):
        return remote(ph_slot(chan, core), along(step), z_send_sem.at[step], z_recv_sem.at[step])

    def source(step):
        return lax.rem(hi + n_hi - step, n_hi)

    def y_copy(step):
        return remote(
            ph_slot(source(step) * 2 + lo, core), beside, y_send_sem.at[step], y_recv_sem.at[step]
        )

    def p_copy(step, other):
        owner = source(step) * 2 + lo + other * (1 - 2 * lo)
        return remote(
            ph_slot(owner, core), sibling, p_send_sem.at[other, step], p_recv_sem.at[other, step]
        )

    @pl.loop(1, n_hi)
    def _(step):
        z_copy(step).start()

    y_copy(0).start()

    def sib_copy(j):
        return pltpu.make_async_remote_copy(
            src_ref=part.at[j, pl.ds(0, chunk)],
            dst_ref=sib_buf.at[j],
            send_sem=sib_send_sem.at[j],
            recv_sem=sib_recv_sem.at[j],
            device_id=sibling,
            device_id_type=MESH,
        )

    def x_copy(i):
        return pltpu.make_async_remote_copy(
            src_ref=x_send.at[i],
            dst_ref=x_recv.at[i],
            send_sem=x_send_sem.at[i],
            recv_sem=x_recv_sem.at[i],
            device_id=across,
            device_id_type=MESH,
        )

    @pl.loop(0, 2 * n_chunk)
    def _(j):
        w_copy(j, 0).wait()
        w_copy(j, 1).wait()
        part[j] = jnp.dot(wbuf[j], low[...], preferred_element_type=jnp.float32)
        sib_copy(j).start()

        @pl.when((j >= 1) & (j <= n_chunk))
        def _():
            i = j - 1
            sib_copy(i).wait_recv()
            x_send[i] = (part[i, pl.ds(chunk, chunk)] + sib_buf[i]).astype(jnp.bfloat16)
            x_copy(i).start()

    @pl.loop(1, n_hi)
    def _(step):
        z_copy(step).wait_recv()
        y_copy(step).start()
        p_copy(step, 0).start()

    @pl.loop(0, n_hi)
    def _(step):
        y_copy(step).wait_recv()
        p_copy(step, 1).start()

    @pl.loop(1, n_hi)
    def _(step):
        p_copy(step, 0).wait_recv()

    @pl.loop(0, n_hi)
    def _(step):
        p_copy(step, 1).wait_recv()

    per_chunk = chunk // tile

    @pl.loop(0, n_chunk)
    def _(i):
        sib_copy(n_chunk + i).wait_recv()
        for t in range(per_chunk):
            r = i * per_chunk + t
            mask = live_mask(r * tile, tile)
            for h in range(2):
                cols = slice(h * 128, (h + 1) * 128)
                at = pl.ds(r * 2 * tile + h, tile, 2)
                value = amp[at, :]
                x_head, x_rest = split(jnp.where(mask, value, jnp.zeros_like(value)))
                m_head, m_rest = split(ph_all[owner_ref[h, r]])
                dot = functools.partial(jnp.dot, preferred_element_type=jnp.float32)
                cycle = dot(x_head, m_head) + (dot(x_rest, m_head) + dot(x_head, m_rest))
                ladder = (
                    part[n_chunk + i, chunk + t * tile : chunk + (t + 1) * tile, cols]
                    + sib_buf[n_chunk + i, t * tile : (t + 1) * tile, cols]
                )
                out[at, :] = jnp.where(mask, ladder, jnp.zeros_like(ladder)) + cycle

    def out_copy(i):
        window = pl.ds(pl.multiple_of(i * 2 * chunk, 2 * chunk), 2 * chunk)
        return pltpu.make_async_copy(out.at[window], out_hbm.at[window], out_sem.at[i])

    @pl.loop(0, n_chunk)
    def _(i):
        x_copy(i).wait_recv()
        for t in range(per_chunk):
            r = i * per_chunk + t
            mask = live_mask(r * tile, tile)
            for h in range(2):
                at = pl.ds(r * 2 * tile + h, tile, 2)
                far = x_recv[i, t * tile : (t + 1) * tile, h * 128 : (h + 1) * 128]
                far = far.astype(jnp.float32)
                out[at, :] += jnp.where(mask, far, jnp.zeros_like(far))
        out_copy(i).start()

    @pl.loop(0, 2 * n_chunk)
    def _(j):
        sib_copy(j).wait_send()

    @pl.loop(0, n_chunk)
    def _(i):
        x_copy(i).wait_send()

    @pl.loop(1, n_hi)
    def _(step):
        z_copy(step).wait_send()
        p_copy(step, 0).wait_send()

    @pl.loop(0, n_hi)
    def _(step):
        y_copy(step).wait_send()
        p_copy(step, 1).wait_send()

    @pl.loop(0, n_chunk)
    def _(i):
        out_copy(i).wait()


def local(n_chan, amplitudes, pair_interaction, ph_interaction, pp_size, ph_owner):
    rows, _, width = amplitudes.shape
    tiles = ph_owner.shape[0]
    per_owner, depth, _ = ph_interaction.shape
    whole_rows = pair_interaction.shape[1]
    tile = rows // tiles
    chunk = 3 * tile
    n_chunk = rows // chunk
    n_hi = n_chan // 2
    dims = (n_hi, n_chunk, chunk, rows, tile, tiles, per_owner)
    dma = pltpu.SemaphoreType.DMA
    any_space = pl.BlockSpec(memory_space=pl.ANY)
    smem = pl.BlockSpec(memory_space=pltpu.SMEM)
    result = pl.pallas_call(
        functools.partial(kernel, dims),
        out_shape=jax.ShapeDtypeStruct((2 * rows, 128), jnp.float32),
        in_specs=[smem, smem, any_space, any_space, any_space],
        out_specs=any_space,
        scratch_shapes=[
            pltpu.VMEM((2 * rows, 128), jnp.float32),
            pltpu.VMEM((2 * n_chunk, 2 * chunk, rows), jnp.bfloat16),
            pltpu.VMEM((rows, width), jnp.bfloat16),
            pltpu.VMEM((2 * n_chunk, 2 * chunk, width), jnp.float32),
            pltpu.VMEM((2 * n_chunk, chunk, width), jnp.float32),
            pltpu.VMEM((n_chunk, chunk, width), jnp.bfloat16),
            pltpu.VMEM((n_chunk, chunk, width), jnp.bfloat16),
            pltpu.VMEM((n_chan * per_owner, depth, depth), jnp.float32),
            pltpu.VMEM((2 * rows, 128), jnp.float32),
            dma,
            dma((2 * n_chunk, 2)),
            dma,
            dma((n_chunk,)),
            dma((2 * n_chunk,)),
            dma((2 * n_chunk,)),
            dma((n_chunk,)),
            dma((n_chunk,)),
            dma((n_hi,)),
            dma((n_hi,)),
            dma((n_hi,)),
            dma((n_hi,)),
            dma((2, n_hi)),
            dma((2, n_hi)),
        ],
        compiler_params=pltpu.CompilerParams(
            collective_id=0, has_side_effects=True, vmem_limit_bytes=48 * 1024 * 1024
        ),
        cost_estimate=pl.CostEstimate(
            flops=2 * whole_rows * rows * width,
            bytes_accessed=2 * whole_rows * rows + 8 * rows * width,
            transcendentals=0,
        ),
    )(
        pp_size,
        jnp.transpose(ph_owner, (1, 2, 0)).reshape(2, tiles),
        amplitudes.reshape(2 * rows, 128),
        pair_interaction.reshape(whole_rows, rows),
        ph_interaction,
    )
    return result.reshape(rows, 1, width)


def solution(mesh):
    in_specs = (
        P("ctr", "chan", None),
        P("chan", None, "ctr"),
        P("chan", None, None),
        P("chan"),
        P("ctr", "chan", None),
    )
    return jax.shard_map(
        functools.partial(local, mesh.shape["chan"]),
        mesh=mesh,
        in_specs=in_specs,
        out_specs=P("ctr", "chan", None),
        check_vma=False,
    )
```

time: 175 us -> 29.9 us (0.17)
  waiting for transfers between devices: 109 us -> 0 us
  Pallas kernels: 0 us -> 25.2 us
  matrix products: 17.9 us -> 0 us
  starting transfers between devices: 16.7 us -> 0 us
  between operations: 14.2 us -> 0.67 us
  local copies, waits for them, and re-layouts: 15.1 us -> 3.86 us
  other arithmetic: 1.84 us -> 0 us
    all_to_all x3 -> x0, waiting for transfers between devices: 109 us -> none  [the longest x1 54 us: local(): lax.all_to_all(result, 'chan', split_axis=0, concat_axis=0, tiled=True)]
    pallas_call x0 -> x1, Pallas kernels: none -> 25.2 us  [local(): pl.pallas_call(functools.partial(kernel, dims), out_shape=jax.ShapeDtypeS...]
    dot_general x3 -> x0, matrix products: 17.9 us -> none  [the longest x1 12.3 us: local(): jnp.einsum('crk,kch->rch', pair_interaction, lowered, preferred_element_t...]
    all_to_all x3 -> x0, starting transfers between devices: 16.7 us -> none  [the longest x1 7.28 us: local(): lax.all_to_all(channel_ids, 'chan', split_axis=0, concat_axis=0, tiled=True)]
    scatter x2 -> x0, local copies, waits for them, and re-layouts: 2.95 us -> none  [the longest x1 2.26 us: local(): jnp.zeros((chan_size * capacity, tile_rows, tile_cols), jnp.float32)]
    reshape x3 -> x0, local copies, waits for them, and re-layouts: 2.13 us -> none  [the longest x1 1.95 us: local(): jnp.transpose(cycle, (0, 3, 1, 2, 4))]
    add x1 -> x0, local copies, waits for them, and re-layouts: 2.1 us -> none  [local(): jnp.where(live_mask[:, :, None], ladder, jnp.zeros_like(ladder)) + cycle]
    select_n x1 -> x0, local copies, waits for them, and re-layouts: 1.94 us -> none  [local(): jnp.where(live_mask[:, :, None], amplitudes, jnp.zeros_like(amplitudes))]
  transfers between devices with their start and end apart: 4 -> 0, of which waited for: 3 -> 0; matrix products, arithmetic and copies ran while one was open for 9% -> 0% of each run, Pallas kernels for 0% -> 0%
where the time goes in v1:
time: 29.9 us; the launch traced here: 29.8 us
  Pallas kernels  25.2 us (84%)
  local copies, waits for them, and re-layouts  3.86 us (13%)
  between operations  0.67 us (2%)
    pallas_call x1, Pallas kernels, local(): pl.pallas_call(functools.partial(kernel, dims), out_shape=jax.ShapeDtypeS...  25.2 us
    unnamed x7, local copies, waits for them, and re-layouts  3.86 us

profile of v1, /device:TPU:0, one launch (start us, length us, event | category | flops | bytes accessed | tf_op | source)
XLA Modules:
  0.0 29.8 jit_solution(9951358008667369287)
XLA Ops:
  0.7 0.0 copy-start
  0.7 1.3 %copy-done = f32[1152,1,256]{2,1,0:T(1,128)S(1)} copy-done((f32[1152,1,256]{2,1,0:T(1,128)S(1)}, f32[1152,1,256]{2,1,0:T(1,128)}, u32[]{:S(2)}) %copy-start) | copy-done | bytes 1179672
  1.9 0.0 copy-start.1
  1.9 0.9 %copy-done.1 = f32[2,128,128]{2,1,0:T(8,128)S(1)} copy-done((f32[2,128,128]{2,1,0:T(8,128)S(1)}, f32[2,128,128]{2,1,0:T(8,128)}, u32[]{:S(2)}) %copy-start.1) | copy-done | bytes 131096
  2.8 0.0 copy-start.2
  2.8 0.7 %copy-done.2 = s32[18,1,2]{0,2,1:T(2,128)S(1)} copy-done((s32[18,1,2]{0,2,1:T(2,128)S(1)}, s32[18,1,2]{0,2,1:T(2,128)}, u32[]{:S(2)}) %copy-start.2) | copy-done | bytes 168
  3.5 25.2 %shard_map.55 = f32[2304,128]{1,0:T(8,128)S(1)} custom-call(s32[1]{0:T(128)S(6)} %copy.8.size_ref, s32[2,18]{1,0:T(2,128)S(1)} %bitcast.8, f32[2304,128]{1,0:T(8,128)S(1)} %bitcast.7, bf16[4608,1152]{1,0:T(8,128)(2,1)} %bitcast.9, f32[2,128,128]{2,1,0:T(8,128)S(1)} %copy-done.1), custom_call_target="tpu_custom_call" | custom-call | flops 2717908992 | bytes 12976128 | tf_op jit(solution)/shard_map/pallas_call | solution.py:277
  28.7 1.0 %copy.9 = f32[1152,1,256]{2,1,0:T(1,128)} copy(f32[1152,1,256]{2,1,0:T(1,128)S(1)} %bitcast.6) | data formatting | bytes 2359296
Async XLA Ops:
  0.7 1.3 %copy-start = (f32[1152,1,256]{2,1,0:T(1,128)S(1)}, f32[1152,1,256]{2,1,0:T(1,128)}, u32[]{:S(2)}) copy-start(f32[1152,1,256]{2,1,0:T(1,128)} %param.5) | copy-start | bytes 3538948
  1.9 0.9 %copy-start.1 = (f32[2,128,128]{2,1,0:T(8,128)S(1)}, f32[2,128,128]{2,1,0:T(8,128)}, u32[]{:S(2)}) copy-start(f32[2,128,128]{2,1,0:T(8,128)} %ph_hbm.1) | copy-start | bytes 393220
  2.8 0.7 %copy-start.2 = (s32[18,1,2]{0,2,1:T(2,128)S(1)}, s32[18,1,2]{0,2,1:T(2,128)}, u32[]{:S(2)}) copy-start(s32[18,1,2]{0,2,1:T(2,128)} %param.9) | copy-start | bytes 436
